TPU v7x, 32 devices: a whole 2x2x4 slice. The times are simulated.
32 devices in a mesh: replica: 8 (over y, x, core), fsdp: 4 (over z).
Axes of the slice: x: 2, y: 2, z: 4, core: 2. Of those that a mesh axis runs over, the one named last changes fastest.
Arguments:
- acts: bfloat16 [4096, 5120], P(('replica', 'fsdp')), may hold values from -6 to 6
- cotangent: bfloat16 [4096, 384], P(('replica', 'fsdp')), may hold values from -6 to 6
- inner_weight: bfloat16 [5120, 384], P('fsdp'), may hold values from -1.5 to 1.5
- outer_weight: float32 [5120, 384], P('fsdp'), may hold values from -1.5 to 1.5
- momentum: float32 [5120, 384], P('fsdp'), may hold values from -1.5 to 1.5
Outputs:
- input_grad: bfloat16 [4096, 5120], P(('replica', 'fsdp'))
- new_outer: float32 [5120, 384], P('fsdp')
- new_momentum: float32 [5120, 384], P('fsdp')
- new_inner: bfloat16 [5120, 384], P('fsdp')
All inputs are finite; a program needn't handle non-finite values.
Results may differ from a plain program's by a relative error of at most 0.015.
Values may be sent and summed in bfloat16 or wider, within the bound.
A program may use at most 64 MiB of HBM per device.

v0:
```python
import jax
import jax.numpy as jnp
from jax import lax
from jax.sharding import PartitionSpec as P

lr_inner = 4.0
beta = 0.9
lr_outer = 0.7


def contract_rows(left, right):
    return lax.dot_general(
        left, right, (((0,), (0,)), ((), ())), preferred_element_type=jnp.float32
    )


def outer_update(delta_mean, outer_rows, moment_rows):
    moment_next = beta * moment_rows + delta_mean
    outer_next = outer_rows - lr_outer * (delta_mean + beta * moment_next)
    return (outer_next, moment_next)


def per_device(acts, cotangent, inner_weight, outer_weight, momentum):
    width = acts.shape[1]
    scale = 1.0 / width**0.5
    gathered = lax.all_gather(inner_weight, "fsdp", axis=0, tiled=True)
    pre = jnp.dot(acts, gathered, preferred_element_type=jnp.float32) * scale
    sig = jax.nn.sigmoid(pre)
    grad_pre = (cotangent.astype(jnp.float32) * sig * (1.0 + pre * (1.0 - sig))).astype(
        jnp.bfloat16
    )
    input_grad = (jnp.dot(grad_pre, gathered.T, preferred_element_type=jnp.float32) * scale).astype(
        jnp.bfloat16
    )
    replicas = lax.axis_size("replica")
    term = contract_rows(acts, grad_pre) * scale
    weight_grad = lax.psum_scatter(
        term.astype(jnp.bfloat16).astype(jnp.float32).astype(jnp.bfloat16),
        "fsdp",
        scatter_dimension=0,
        tiled=True,
    ).astype(jnp.float32)
    delta = outer_weight - (inner_weight.astype(jnp.float32) - lr_inner * weight_grad)
    total = lax.psum(delta, "replica")
    new_outer, new_momentum = outer_update(total / replicas, outer_weight, momentum)
    return (input_grad, new_outer, new_momentum, new_outer.astype(jnp.bfloat16))


def solution(mesh):
    placed = (
        P(("replica", "fsdp"), None),
        P(("replica", "fsdp"), None),
        P("fsdp", None),
        P("fsdp", None),
        P("fsdp", None),
    )
    return jax.shard_map(
        per_device,
        mesh=mesh,
        in_specs=placed,
        out_specs=(P(("replica", "fsdp"), None), P("fsdp", None), P("fsdp", None), P("fsdp", None)),
        check_vma=False,
    )
```

profile of v0, /device:TPU:1, one launch (start us, length us, event | category | flops | bytes accessed | tf_op | source)
XLA Modules:
  0.0 248.2 jit_solution(1000286068400042586)
XLA Ops:
  7.2 0.0 copy-start
  7.2 0.0 all-gather.2.cloned.1.call-start
  7.2 0.7 all-gather.2.cloned.1.call-update
  7.9 0.0 copy-start.3
  7.9 0.0 reduce-scatter.2.cloned.1.call-start
  8.0 80.2 %all-gather.2.cloned.1.call-done = bf16[5120,384]{1,0:T(8,128)(2,1)} async-done(((bf16[1280,384]{1,0:T(8,128)(2,1)}), bf16[5120,384]{1,0:T(8,128)(2,1)}) %all-gather.2.cloned.1.call-update) | async-done | bytes 3932176 | tf_op jit(solution)/shard_map/all_gather | solution.py:26
  88.2 0.0 copy-done
  88.2 3.0 %convolution_multiply_fusion.1 = f32[128,384]{1,0:T(8,128)S(1)} fusion(bf16[128,5120]{1,0:T(8,128)(2,1)S(1)} %copy-done, bf16[5120,384]{1,0:T(8,128)(2,1)} %all-gather.2.cloned.1.call-done), kind=kOutput, calls=%fused_computation.7 | convolution fusion | flops 503365632 | bytes 5439488 | tf_op jit(solution)/shard_map/dot_general | solution.py:27
  91.1 0.0 copy-done.3
  91.1 3.1 %fusion = bf16[5120,384]{0,1:T(8,128)(2,1)} fusion(bf16[128,5120]{1,0:T(8,128)(2,1)S(1)} %copy-done, f32[128,384]{1,0:T(8,128)S(1)} %convolution_multiply_fusion.1, bf16[128,384]{1,0:T(8,128)(2,1)S(1)} %copy-done.3), kind=kOutput, calls=%fused_computation.1 | convolution fusion | flops 507740160 | bytes 5537792 | tf_op jit(solution)/shard_map/dot_general | solution.py:12
  94.2 0.0 copy-start.2
  94.2 0.0 reduce-scatter.2.cloned.1.call-update
  94.3 0.0 all-reduce.2.cloned.1.call-start
  94.3 1.1 copy-done.2
  95.5 1.3 copy.9
  96.8 1.9 copy.12
  98.7 66.6 %reduce-scatter.2.cloned.1.call-done = bf16[1280,384]{0,1:T(8,128)(2,1)} async-done(((bf16[5120,384]{0,1:T(8,128)(2,1)}), bf16[1280,384]{0,1:T(8,128)(2,1)}) %reduce-scatter.2.cloned.1.call-update) | async-done | bytes 983056 | tf_op jit(solution)/shard_map/reduce_scatter | solution.py:37
  165.3 3.1 %subtract_subtract_fusion = f32[1280,384]{0,1:T(8,128)} fusion(f32[1280,384]{0,1:T(8,128)S(1)} %copy.12, bf16[1280,384]{0,1:T(8,128)(2,1)} %reduce-scatter.2.cloned.1.call-done, bf16[1280,384]{0,1:T(8,128)(2,1)} %copy.9), kind=kLoop, calls=%fused_computation.6 | loop fusion | flops 2457600 | bytes 5898240 | tf_op jit(solution)/shard_map/sub | solution.py:43
  168.4 0.0 all-reduce.2.cloned.1.call-update
  168.4 2.8 %copy.11 = f32[1280,384]{0,1:T(8,128)} copy(f32[1280,384]{1,0:T(8,128)} %param.9) | data formatting | bytes 3932160 | tf_op args[4]
  171.2 4.6 %fusion.1 = bf16[128,5120]{1,0:T(8,128)(2,1)} fusion(bf16[5120,384]{1,0:T(8,128)(2,1)} %all-gather.2.cloned.1.call-done, f32[128,384]{1,0:T(8,128)S(1)} %convolution_multiply_fusion.1, bf16[128,384]{1,0:T(8,128)(2,1)} %param.6), kind=kOutput, calls=%fused_computation.3 | convolution fusion | flops 505118720 | bytes 5537792 | tf_op jit(solution)/shard_map/dot_general | solution.py:32
  175.8 53.9 %all-reduce.2.cloned.1.call-done = f32[1280,384]{0,1:T(8,128)} async-done(((f32[1280,384]{0,1:T(8,128)}), f32[1280,384]{0,1:T(8,128)}) %all-reduce.2.cloned.1.call-update) | async-done | bytes 1966096 | tf_op jit(solution)/shard_map/psum | solution.py:44
  229.8 4.9 %fusion.8 = (bf16[1280,384]{0,1:T(8,128)(2,1)}, f32[1280,384]{0,1:T(8,128)}, f32[1280,384]{0,1:T(8,128)}) fusion(f32[1280,384]{0,1:T(8,128)S(1)} %copy.12, f32[1280,384]{0,1:T(8,128)} %copy.11, f32[1280,384]{0,1:T(8,128)} %all-reduce.2.cloned.1.call-done), kind=kLoop, calls=%fused_computation.15 | loop fusion | flops 3932160 | bytes 10813440 | tf_op jit(solution)/shard_map/convert_element_type | solution.py:46
  234.7 0.0 copy-start.1
  234.7 3.0 %copy.13 = f32[1280,384]{1,0:T(8,128)} copy(f32[1280,384]{0,1:T(8,128)} %get-tuple-element.9) | data formatting | bytes 3932160
  237.7 0.0 copy-done.1
  237.7 1.8 copy.14
  239.5 2.2 copy.15
Async XLA Ops:
  7.2 81.0 %copy-start = (bf16[128,5120]{1,0:T(8,128)(2,1)S(1)}, bf16[128,5120]{1,0:T(8,128)(2,1)}, u32[]{:S(2)}) copy-start(bf16[128,5120]{1,0:T(8,128)(2,1)} %param.5) | copy-start | bytes 3932164
  7.2 81.0 %all-gather.2.cloned.1.call-start = ((), (), s32[]{:S(2)}) async-start(), calls=%async_computation.1 | async-start | bytes 4915200 | tf_op jit(solution)/shard_map/all_gather | solution.py:26
  7.9 83.2 %copy-start.3 = (bf16[128,384]{1,0:T(8,128)(2,1)S(1)}, bf16[128,384]{1,0:T(8,128)(2,1)}, u32[]{:S(2)}) copy-start(bf16[128,384]{1,0:T(8,128)(2,1)} %param.6) | copy-start | bytes 294916
  7.9 157.4 %reduce-scatter.2.cloned.1.call-start = ((), (), s32[]{:S(2)}) async-start(), calls=%async_computation.2 | async-start | bytes 4915200 | tf_op jit(solution)/shard_map/reduce_scatter | solution.py:37
  94.2 1.2 copy-start.2
  94.3 135.5 %all-reduce.2.cloned.1.call-start = ((), (), s32[]{:S(2)}) async-start(), calls=%async_computation.3 | async-start | bytes 3932160 | tf_op jit(solution)/shard_map/psum | solution.py:44
  234.7 3.0 %copy-start.1 = (f32[1280,384]{0,1:T(8,128)S(1)}, f32[1280,384]{0,1:T(8,128)}, u32[]{:S(2)}) copy-start(f32[1280,384]{0,1:T(8,128)} %get-tuple-element.10) | copy-start | bytes 5898244
Sparse Core Ops, SparseCore 0:
  9.6 78.5 all-gather.1
  94.4 70.8 reduce-scatter.1
  169.2 60.5 all-reduce.1
where the time goes:
time: 250 us; the launch traced here: 248 us
  waiting for transfers between devices  201 us (80%)
  local copies, waits for them, and re-layouts  14.1 us (6%)
  between operations  13.8 us (6%)
  matrix products  10.7 us (4%)
  other arithmetic  8.03 us (3%)
    all_gather x1, waiting for transfers between devices, per_device(): gathered = lax.all_gather(inner_weight, 'fsdp', axis=0, tiled=True)  80.2 us
    reduce_scatter x1, waiting for transfers between devices, per_device(): lax.psum_scatter(term.astype(jnp.bfloat16).astype(jnp.float32).astype(jnp...  66.6 us
    psum x1, waiting for transfers between devices, per_device(): total = lax.psum(delta, 'replica')  53.9 us
    unnamed x14, local copies, waits for them, and re-layouts  14.1 us
  transfers between devices with their start and end apart: 3, of which 3 were waited for; matrix products, arithmetic and copies ran while one was open for 4% of the time, Pallas kernels for 0%

commit v1 on v0

--- a/solution.py
+++ b/solution.py
@@ -1,11 +1,17 @@
+import functools
+
 import jax
 import jax.numpy as jnp
 from jax import lax
+from jax.experimental import pallas as pl
+from jax.experimental.pallas import tpu as pltpu
 from jax.sharding import PartitionSpec as P
 
 lr_inner = 4.0
 beta = 0.9
 lr_outer = 0.7
+
+MESH = pl.DeviceIdType.MESH
 
 
 def contract_rows(left, right):
@@ -20,7 +26,266 @@
     return (outer_next, moment_next)
 
 
-def per_device(acts, cotangent, inner_weight, outer_weight, momentum):
+def kernel(
+    n_fsdp,
+    acts_hbm,
+    cot_hbm,
+    w_hbm,
+    ig_hbm,
+    g_hbm,
+    acts,
+    cot,
+    acts_t,
+    w_all,
+    ig,
+    sib_out,
+    sib_in,
+    half_sum,
+    plane_in,
+    shard_out,
+    shard_in,
+    total,
+    local_sem,
+    wz_s,
+    wz_r,
+    wp_s,
+    wp_r,
+    wc_s,
+    wc_r,
+    tc_s,
+    tc_r,
+    tp_s,
+    tp_r,
+    tz_s,
+    tz_r,
+    gp_s,
+    gp_r,
+    gc_s,
+    gc_r,
+):
+    me = lax.axis_index("replica")
+    z = lax.axis_index("fsdp")
+    rows = w_hbm.shape[0]
+    half = rows // 2
+    sub = half // 4
+    width = acts.shape[1]
+    scale = 1.0 / width**0.5
+    chip, core = me // 2, me % 2
+    x, y = chip % 2, chip // 2
+    chips = ((1 - y) * 2 + 1 - x, y * 2 + 1 - x, (1 - y) * 2 + x)
+    sibling = (chip * 2 + 1 - core, z)
+    peers = [(q * 2 + core, z) for q in chips]
+    steps = range(1, n_fsdp)
+    above = [(z + j) % n_fsdp for j in range(n_fsdp)]
+    below = [(z + n_fsdp - j) % n_fsdp for j in range(n_fsdp)]
+
+    def at(ref, start, size):
+        return ref.at[pl.ds(pl.multiple_of(start, 16), size)]
+
+    def remote(src, dst, s, r, dev):
+        return pltpu.make_async_remote_copy(
+            src_ref=src, dst_ref=dst, send_sem=s, recv_sem=r, device_id=dev, device_id_type=MESH
+        )
+
+    loads = [
+        pltpu.make_async_copy(w_hbm, at(w_all, z * rows, rows), local_sem.at[0]),
+        pltpu.make_async_copy(acts_hbm, acts, local_sem.at[1]),
+        pltpu.make_async_copy(cot_hbm, cot, local_sem.at[2]),
+    ]
+    for load in loads:
+        load.start()
+
+    barrier = pltpu.get_barrier_semaphore()
+    partners = [(me, above[j]) for j in steps] + peers + [sibling]
+    for dev in partners:
+        pl.semaphore_signal(barrier, inc=1, device_id=dev, device_id_type=MESH)
+    pl.semaphore_wait(barrier, len(partners))
+
+    sent = []
+
+    def send(src, dst, s, r, dev):
+        copy = remote(src, dst, s, r, dev)
+        copy.start()
+        sent.append(copy)
+
+    def arrived(landing, s, r, dev):
+        remote(landing, landing, s, r, dev).wait_recv()
+
+    mine = core * half + chip * sub
+    for j in steps:
+        send(
+            at(w_hbm, mine, sub),
+            at(w_all, z * rows + mine, sub),
+            wz_s.at[j - 1],
+            wz_r.at[j - 1],
+            (me, above[j]),
+        )
+    for load in loads:
+        load.wait()
+
+    def partial_pre(start, size):
+        start = pl.multiple_of(start, 128)
+        return jnp.dot(
+            acts[:, pl.ds(start, size)],
+            w_all[pl.ds(start, size), :],
+            preferred_element_type=jnp.float32,
+        )
+
+    for j in steps:
+        piece = at(w_all, below[j] * rows + mine, sub)
+        arrived(piece, wz_s.at[j - 1], wz_r.at[j - 1], (me, above[j]))
+        for k in range(3):
+            send(piece, piece, wp_s.at[j - 1, k], wp_r.at[j - 1, k], peers[k])
+
+    pre = partial_pre(z * rows, rows)
+    for b in range(width // half):
+        acts_t[b * half : (b + 1) * half, :] = acts[:, b * half : (b + 1) * half].T
+
+    for j in steps:
+        start = below[j] * rows + core * half
+        for k in range(3):
+            piece = at(w_all, start + chips[k] * sub, sub)
+            arrived(piece, wp_s.at[j - 1, k], wp_r.at[j - 1, k], peers[k])
+        piece = at(w_all, start, half)
+        send(piece, piece, wc_s.at[j - 1], wc_r.at[j - 1], sibling)
+        pre += partial_pre(start, half)
+    for j in steps:
+        start = below[j] * rows + (1 - core) * half
+        arrived(at(w_all, start, half), wc_s.at[j - 1], wc_r.at[j - 1], sibling)
+        pre += partial_pre(start, half)
+
+    pre = pre * scale
+    sig = jax.nn.sigmoid(pre)
+    grad_pre = (cot[...].astype(jnp.float32) * sig * (1.0 + pre * (1.0 - sig))).astype(
+        jnp.bfloat16
+    )
+
+    def term(start):
+        block = acts_t[pl.ds(pl.multiple_of(start, 128), half), :]
+        return jnp.dot(block, grad_pre, preferred_element_type=jnp.float32) * scale
+
+    order = [j % n_fsdp for j in range(1, n_fsdp + 1)]
+    for i, j in enumerate(order):
+        sib_out[i] = term(above[j] * rows + (1 - core) * half).astype(jnp.bfloat16)
+        send(sib_out.at[i], sib_in.at[i], tc_s.at[i], tc_r.at[i], sibling)
+    for i, j in enumerate(order):
+        own = term(above[j] * rows + core * half)
+        arrived(sib_in.at[i], tc_s.at[i], tc_r.at[i], sibling)
+        half_sum[i] = (own + sib_in[i].astype(jnp.float32)).astype(jnp.bfloat16)
+        for k in range(3):
+            send(
+                at(half_sum.at[i], chips[k] * sub, sub),
+                plane_in.at[i, k],
+                tp_s.at[i, k],
+                tp_r.at[i, k],
+                peers[k],
+            )
+    stores = []
+    for i, j in enumerate(order):
+        c0, c1 = i * rows, (i + 1) * rows
+        ig[:, c0:c1] = (
+            lax.dot_general(
+                grad_pre,
+                w_all[c0:c1, :],
+                (((1,), (1,)), ((), ())),
+                preferred_element_type=jnp.float32,
+            )
+            * scale
+        ).astype(jnp.bfloat16)
+        store = pltpu.make_async_copy(
+            ig.at[:, c0:c1], ig_hbm.at[:, c0:c1], local_sem.at[3 + i]
+        )
+        store.start()
+        stores.append(store)
+        acc = half_sum[i, pl.ds(pl.multiple_of(chip * sub, 16), sub), :].astype(jnp.float32)
+        for k in range(3):
+            arrived(plane_in.at[i, k], tp_s.at[i, k], tp_r.at[i, k], peers[k])
+            acc += plane_in[i, k].astype(jnp.float32)
+        if j:
+            shard_out[i] = acc.astype(jnp.bfloat16)
+            send(shard_out.at[i], shard_in.at[i], tz_s.at[i], tz_r.at[i], (me, above[j]))
+    for i in range(n_fsdp - 1):
+        arrived(shard_in.at[i], tz_s.at[i], tz_r.at[i], (me, above[order[i]]))
+        acc += shard_in[i].astype(jnp.float32)
+
+    total[pl.ds(pl.multiple_of(mine, 16), sub), :] = acc.astype(jnp.bfloat16)
+    piece = at(total, mine, sub)
+    for k in range(3):
+        send(piece, piece, gp_s.at[k], gp_r.at[k], peers[k])
+    send(piece, piece, gc_s.at[3], gc_r.at[3], sibling)
+    for k in (1, 2, 0):
+        piece = at(total, core * half + chips[k] * sub, sub)
+        arrived(piece, gp_s.at[k], gp_r.at[k], peers[k])
+        send(piece, piece, gc_s.at[k], gc_r.at[k], sibling)
+    for k in (3, 1, 2, 0):
+        q = chip if k == 3 else chips[k]
+        arrived(at(total, (1 - core) * half + q * sub, sub), gc_s.at[k], gc_r.at[k], sibling)
+    last = pltpu.make_async_copy(total, g_hbm, local_sem.at[3 + n_fsdp])
+    last.start()
+    for copy in sent:
+        copy.wait_send()
+    for store in stores:
+        store.wait()
+    last.wait()
+
+
+def fused(acts, cotangent, inner_weight, n_fsdp):
+    tok, width = acts.shape
+    rows, cols = inner_weight.shape
+    half, sub = rows // 2, rows // 8
+    bf = jnp.bfloat16
+    dma = pltpu.SemaphoreType.DMA
+    s = n_fsdp - 1
+    anywhere = pl.BlockSpec(memory_space=pl.ANY)
+    return pl.pallas_call(
+        functools.partial(kernel, n_fsdp),
+        out_shape=(
+            jax.ShapeDtypeStruct((tok, width), bf),
+            jax.ShapeDtypeStruct((rows, cols), bf),
+        ),
+        in_specs=[anywhere] * 3,
+        out_specs=(anywhere, anywhere),
+        scratch_shapes=[
+            pltpu.VMEM((tok, width), bf),
+            pltpu.VMEM((tok, cols), bf),
+            pltpu.VMEM((width, tok), bf),
+            pltpu.VMEM((width, cols), bf),
+            pltpu.VMEM((tok, width), bf),
+            pltpu.VMEM((n_fsdp, half, cols), bf),
+            pltpu.VMEM((n_fsdp, half, cols), bf),
+            pltpu.VMEM((n_fsdp, half, cols), bf),
+            pltpu.VMEM((n_fsdp, 3, sub, cols), bf),
+            pltpu.VMEM((s, sub, cols), bf),
+            pltpu.VMEM((s, sub, cols), bf),
+            pltpu.VMEM((rows, cols), bf),
+            dma((4 + n_fsdp,)),
+            dma((s,)),
+            dma((s,)),
+            dma((s, 3)),
+            dma((s, 3)),
+            dma((s,)),
+            dma((s,)),
+            dma((n_fsdp,)),
+            dma((n_fsdp,)),
+            dma((n_fsdp, 3)),
+            dma((n_fsdp, 3)),
+            dma((s,)),
+            dma((s,)),
+            dma((3,)),
+            dma((3,)),
+            dma((4,)),
+            dma((4,)),
+        ],
+        compiler_params=pltpu.CompilerParams(
+            collective_id=0, has_side_effects=True, vmem_limit_bytes=48 * 2**20
+        ),
+        cost_estimate=pl.CostEstimate(
+            flops=6 * tok * width * cols, bytes_accessed=4 * tok * width, transcendentals=0
+        ),
+    )(acts, cotangent, inner_weight)
+
+
+def by_collectives(acts, cotangent, inner_weight):
     width = acts.shape[1]
     scale = 1.0 / width**0.5
     gathered = lax.all_gather(inner_weight, "fsdp", axis=0, tiled=True)
@@ -32,17 +297,25 @@
     input_grad = (jnp.dot(grad_pre, gathered.T, preferred_element_type=jnp.float32) * scale).astype(
         jnp.bfloat16
     )
-    replicas = lax.axis_size("replica")
     term = contract_rows(acts, grad_pre) * scale
     weight_grad = lax.psum_scatter(
-        term.astype(jnp.bfloat16).astype(jnp.float32).astype(jnp.bfloat16),
-        "fsdp",
-        scatter_dimension=0,
-        tiled=True,
+        term.astype(jnp.bfloat16), "fsdp", scatter_dimension=0, tiled=True
     ).astype(jnp.float32)
-    delta = outer_weight - (inner_weight.astype(jnp.float32) - lr_inner * weight_grad)
-    total = lax.psum(delta, "replica")
-    new_outer, new_momentum = outer_update(total / replicas, outer_weight, momentum)
+    return input_grad, lax.psum(weight_grad, "replica")
+
+
+def per_device(acts, cotangent, inner_weight, outer_weight, momentum):
+    replicas = lax.axis_size("replica")
+    n_fsdp = lax.axis_size("fsdp")
+    rows = inner_weight.shape[0]
+    if replicas == 8 and rows % 256 == 0 and n_fsdp > 1:
+        input_grad, grad_sum = fused(acts, cotangent, inner_weight, n_fsdp)
+    else:
+        input_grad, grad_sum = by_collectives(acts, cotangent, inner_weight)
+    delta_mean = (outer_weight - inner_weight.astype(jnp.float32)) + (
+        lr_inner / replicas
+    ) * grad_sum.astype(jnp.float32)
+    new_outer, new_momentum = outer_update(delta_mean, outer_weight, momentum)
     return (input_grad, new_outer, new_momentum, new_outer.astype(jnp.bfloat16))
 
 

time: 250 us -> 71.9 us (0.29)
  waiting for transfers between devices: 201 us -> 0 us
  Pallas kernels: 0 us -> 63.6 us
  between operations: 13.8 us -> 0.67 us
  matrix products: 10.7 us -> 0 us
  local copies, waits for them, and re-layouts: 14.1 us -> 4.47 us
  other arithmetic: 8.03 us -> 2.94 us
    all_gather x1 -> x0, waiting for transfers between devices: 80.2 us -> none  [per_device(): gathered = lax.all_gather(inner_weight, 'fsdp', axis=0, tiled=True)]
    reduce_scatter x1 -> x0, waiting for transfers between devices: 66.6 us -> none  [per_device(): lax.psum_scatter(term.astype(jnp.bfloat16).astype(jnp.float32).astype(jnp...]
    pallas_call x0 -> x1, Pallas kernels: none -> 63.6 us  [fused(): pl.pallas_call(functools.partial(kernel, n_fsdp), out_shape=(jax.ShapeDty...]
    psum x1 -> x0, waiting for transfers between devices: 53.9 us -> none  [per_device(): total = lax.psum(delta, 'replica')]
    dot_general x3 -> x0, matrix products: 10.7 us -> none  [the longest x1 4.58 us: per_device(): jnp.dot(grad_pre, gathered.T, preferred_element_type=jnp.float32) * scale]
    unnamed x14 -> x11, local copies, waits for them, and re-layouts: 14.1 us -> 4.47 us
    sub x1 -> x0, other arithmetic: 3.09 us -> none  [per_device(): outer_weight - (inner_weight.astype(jnp.float32) - lr_inner * weight_grad)]
  transfers between devices with their start and end apart: 3 -> 0, of which waited for: 3 -> 0; matrix products, arithmetic and copies ran while one was open for 4% -> 0% of each run, Pallas kernels for 0% -> 0%
where the time goes in v1:
time: 71.9 us; the launch traced here: 71.6 us
  Pallas kernels  63.6 us (88%)
  local copies, waits for them, and re-layouts  4.47 us (6%)
  other arithmetic  2.94 us (4%)
    pallas_call x1, Pallas kernels, fused(): pl.pallas_call(functools.partial(kernel, n_fsdp), out_shape=(jax.ShapeDty...  63.6 us
    unnamed x11, local copies, waits for them, and re-layouts  4.47 us
    convert_element_type x1, other arithmetic, per_device(): return (input_grad, new_outer, new_momentum, new_outer.astype(jnp.bfloat16))  2.94 us

profile of v1, /device:TPU:1, one launch (start us, length us, event | category | flops | bytes accessed | tf_op | source)
XLA Modules:
  0.0 71.6 jit_solution(15617068128271200617)
XLA Ops:
  0.6 0.0 copy-start
  0.6 1.2 %copy-done = bf16[1280,384]{1,0:T(8,128)(2,1)S(1)} copy-done((bf16[1280,384]{1,0:T(8,128)(2,1)S(1)}, bf16[1280,384]{1,0:T(8,128)(2,1)}, u32[]{:S(2)}) %copy-start) | copy-done | bytes 983064
  1.8 0.0 copy-start.1
  1.8 1.3 %copy-done.1 = bf16[128,5120]{1,0:T(8,128)(2,1)S(1)} copy-done((bf16[128,5120]{1,0:T(8,128)(2,1)S(1)}, bf16[128,5120]{1,0:T(8,128)(2,1)}, u32[]{:S(2)}) %copy-start.1) | copy-done | bytes 1310744
  3.2 0.0 copy-start.2
  3.2 0.9 %copy-done.2 = bf16[128,384]{1,0:T(8,128)(2,1)S(1)} copy-done((bf16[128,384]{1,0:T(8,128)(2,1)S(1)}, bf16[128,384]{1,0:T(8,128)(2,1)}, u32[]{:S(2)}) %copy-start.2) | copy-done | bytes 98328
  4.0 0.0 copy-start.3
  4.0 0.0 copy-start.4
  4.0 63.6 %shard_map.84 = (bf16[128,5120]{1,0:T(8,128)(2,1)S(1)}, bf16[1280,384]{1,0:T(8,128)(2,1)S(1)}) custom-call(bf16[128,5120]{1,0:T(8,128)(2,1)S(1)} %copy-done.1, bf16[128,384]{1,0:T(8,128)(2,1)S(1)} %copy-done.2, bf16[1280,384]{1,0:T(8,128)(2,1)S(1)} %copy-done), custom_call_target="tpu_custom_call" | custom-call | flops 1509949440 | bytes 2621440 | tf_op jit(solution)/shard_map/pallas_call | solution.py:240
  67.6 0.0 copy-done.3
  67.6 0.0 copy-done.4
  67.7 2.9 %fusion = (bf16[1280,384]{1,0:T(8,128)(2,1)}, f32[1280,384]{1,0:T(8,128)}, f32[1280,384]{1,0:T(8,128)}) fusion(f32[1280,384]{1,0:T(8,128)S(1)} %copy-done.3, bf16[1280,384]{1,0:T(8,128)(2,1)S(1)} %get-tuple-element.7, bf16[1280,384]{1,0:T(8,128)(2,1)S(1)} %copy-done, f32[1280,384]{1,0:T(8,128)S(1)} %copy-done.4), kind=kLoop, calls=%fused_computation.3 | loop fusion | flops 5898240 | bytes 10813440 | tf_op jit(solution)/shard_map/convert_element_type | solution.py:319
  70.6 1.1 %copy.10 = bf16[128,5120]{1,0:T(8,128)(2,1)} copy(bf16[128,5120]{1,0:T(8,128)(2,1)S(1)} %get-tuple-element.15) | data formatting | bytes 2621440
Async XLA Ops:
  0.6 1.2 %copy-start = (bf16[1280,384]{1,0:T(8,128)(2,1)S(1)}, bf16[1280,384]{1,0:T(8,128)(2,1)}, u32[]{:S(2)}) copy-start(bf16[1280,384]{1,0:T(8,128)(2,1)} %w_hbm.1) | copy-start | bytes 2949124
  1.8 1.3 %copy-start.1 = (bf16[128,5120]{1,0:T(8,128)(2,1)S(1)}, bf16[128,5120]{1,0:T(8,128)(2,1)}, u32[]{:S(2)}) copy-start(bf16[128,5120]{1,0:T(8,128)(2,1)} %acts_hbm.1) | copy-start | bytes 3932164
  3.2 0.9 %copy-start.2 = (bf16[128,384]{1,0:T(8,128)(2,1)S(1)}, bf16[128,384]{1,0:T(8,128)(2,1)}, u32[]{:S(2)}) copy-start(bf16[128,384]{1,0:T(8,128)(2,1)} %cot_hbm.1) | copy-start | bytes 294916
  4.0 63.6 %copy-start.3 = (f32[1280,384]{1,0:T(8,128)S(1)}, f32[1280,384]{1,0:T(8,128)}, u32[]{:S(2)}) copy-start(f32[1280,384]{1,0:T(8,128)} %param.8) | copy-start | bytes 5898244
  4.0 63.6 %copy-start.4 = (f32[1280,384]{1,0:T(8,128)S(1)}, f32[1280,384]{1,0:T(8,128)}, u32[]{:S(2)}) copy-start(f32[1280,384]{1,0:T(8,128)} %param.9) | copy-start | bytes 5898244

commit v2 on v1

--- a/solution.py
+++ b/solution.py
@@ -41,7 +41,10 @@
     sib_out,
     sib_in,
     half_sum,
-    plane_in,
+    first_out,
+    first_in,
+    second_out,
+    second_in,
     shard_out,
     shard_in,
     total,
@@ -72,12 +75,15 @@
     scale = 1.0 / width**0.5
     chip, core = me // 2, me % 2
     x, y = chip % 2, chip // 2
-    chips = ((1 - y) * 2 + 1 - x, y * 2 + 1 - x, (1 - y) * 2 + x)
+    chips = (y * 2 + 1 - x, (1 - y) * 2 + x, (1 - y) * 2 + 1 - x)
     sibling = (chip * 2 + 1 - core, z)
     peers = [(q * 2 + core, z) for q in chips]
-    steps = range(1, n_fsdp)
-    above = [(z + j) % n_fsdp for j in range(n_fsdp)]
-    below = [(z + n_fsdp - j) % n_fsdp for j in range(n_fsdp)]
+    x_peer, y_peer, _ = peers
+    hop = sub // 2
+    near, two, mirror = z + 1 - 2 * (z % 2), (z + 2) % 4, 3 - z
+    middle = (z + z // 2) % 2
+    sources = (near, middle * mirror + (1 - middle) * two, middle * two + (1 - middle) * mirror)
+    targets = (mirror, two, near, z)
 
     def at(ref, start, size):
         return ref.at[pl.ds(pl.multiple_of(start, 16), size)]
@@ -96,7 +102,7 @@
         load.start()
 
     barrier = pltpu.get_barrier_semaphore()
-    partners = [(me, above[j]) for j in steps] + peers + [sibling]
+    partners = [(me, other) for other in targets[:3]] + peers + [sibling]
     for dev in partners:
         pl.semaphore_signal(barrier, inc=1, device_id=dev, device_id_type=MESH)
     pl.semaphore_wait(barrier, len(partners))
@@ -111,15 +117,28 @@
     def arrived(landing, s, r, dev):
         remote(landing, landing, s, r, dev).wait_recv()
 
+    def hand_on(source, up, down, src):
+        piece = at(w_all, source * rows + mine, sub)
+        for way, (cond, other) in enumerate(((up, z + 1), (down, z - 1))):
+
+            @pl.when(cond)
+            def _():
+                remote(
+                    src, piece, wz_s.at[way, source], wz_r.at[source], (me, other)
+                ).start()
+
+    def handed_on(source, up, down):
+        piece = at(w_all, source * rows + mine, sub)
+        for way, (cond, other) in enumerate(((up, z + 1), (down, z - 1))):
+
+            @pl.when(cond)
+            def _():
+                remote(
+                    piece, piece, wz_s.at[way, source], wz_r.at[source], (me, other)
+                ).wait_send()
+
     mine = core * half + chip * sub
-    for j in steps:
-        send(
-            at(w_hbm, mine, sub),
-            at(w_all, z * rows + mine, sub),
-            wz_s.at[j - 1],
-            wz_r.at[j - 1],
-            (me, above[j]),
-        )
+    hand_on(z, z < n_fsdp - 1, z > 0, at(w_hbm, mine, sub))
     for load in loads:
         load.wait()
 
@@ -131,27 +150,47 @@
             preferred_element_type=jnp.float32,
         )
 
-    for j in steps:
-        piece = at(w_all, below[j] * rows + mine, sub)
-        arrived(piece, wz_s.at[j - 1], wz_r.at[j - 1], (me, above[j]))
-        for k in range(3):
-            send(piece, piece, wp_s.at[j - 1, k], wp_r.at[j - 1, k], peers[k])
+    def onward(source):
+        return jnp.logical_and(source < z, z < n_fsdp - 1), jnp.logical_and(source > z, z > 0)
+
+    for t, source in enumerate(sources):
+        piece = at(w_all, source * rows + mine, sub)
+        arrived(piece, wz_s.at[0, source], wz_r.at[source], (me, near))
+        hand_on(source, *onward(source), piece)
+        send(piece, piece, wp_s.at[t, 0], wp_r.at[t, 0], x_peer)
+        send(piece, piece, wp_s.at[t, 1], wp_r.at[t, 1], y_peer)
 
     pre = partial_pre(z * rows, rows)
+
+    def relay(t):
+        start = sources[t] * rows + core * half
+        arrived(at(w_all, start + chips[0] * sub, sub), wp_s.at[t, 0], wp_r.at[t, 0], x_peer)
+        piece = at(w_all, start + chips[0] * sub, hop)
+        send(piece, piece, wp_s.at[t, 3], wp_r.at[t, 3], y_peer)
+        arrived(at(w_all, start + chips[1] * sub, sub), wp_s.at[t, 1], wp_r.at[t, 1], y_peer)
+        piece = at(w_all, start + chips[1] * sub + hop, hop)
+        send(piece, piece, wp_s.at[t, 2], wp_r.at[t, 2], x_peer)
+
+    def use(t):
+        start = sources[t] * rows + core * half
+        diagonal = start + chips[2] * sub
+        arrived(at(w_all, diagonal, hop), wp_s.at[t, 3], wp_r.at[t, 3], y_peer)
+        arrived(at(w_all, diagonal + hop, hop), wp_s.at[t, 2], wp_r.at[t, 2], x_peer)
+        piece = at(w_all, start, half)
+        send(piece, piece, wc_s.at[t], wc_r.at[t], sibling)
+        return partial_pre(start, half)
+
+    relay(0)
     for b in range(width // half):
         acts_t[b * half : (b + 1) * half, :] = acts[:, b * half : (b + 1) * half].T
-
-    for j in steps:
-        start = below[j] * rows + core * half
-        for k in range(3):
-            piece = at(w_all, start + chips[k] * sub, sub)
-            arrived(piece, wp_s.at[j - 1, k], wp_r.at[j - 1, k], peers[k])
-        piece = at(w_all, start, half)
-        send(piece, piece, wc_s.at[j - 1], wc_r.at[j - 1], sibling)
-        pre += partial_pre(start, half)
-    for j in steps:
-        start = below[j] * rows + (1 - core) * half
-        arrived(at(w_all, start, half), wc_s.at[j - 1], wc_r.at[j - 1], sibling)
+    relay(1)
+    pre += use(0)
+    relay(2)
+    pre += use(1)
+    pre += use(2)
+    for t, source in enumerate(sources):
+        start = source * rows + (1 - core) * half
+        arrived(at(w_all, start, half), wc_s.at[t], wc_r.at[t], sibling)
         pre += partial_pre(start, half)
 
     pre = pre * scale
@@ -164,24 +203,56 @@
         block = acts_t[pl.ds(pl.multiple_of(start, 128), half), :]
         return jnp.dot(block, grad_pre, preferred_element_type=jnp.float32) * scale
 
-    order = [j % n_fsdp for j in range(1, n_fsdp + 1)]
-    for i, j in enumerate(order):
-        sib_out[i] = term(above[j] * rows + (1 - core) * half).astype(jnp.bfloat16)
+    for i, target in enumerate(targets):
+        sib_out[i] = term(target * rows + (1 - core) * half).astype(jnp.bfloat16)
         send(sib_out.at[i], sib_in.at[i], tc_s.at[i], tc_r.at[i], sibling)
-    for i, j in enumerate(order):
-        own = term(above[j] * rows + core * half)
+
+    def rows_of(i, q, second):
+        return half_sum[i, pl.ds(pl.multiple_of(q * sub + second * hop, 16), hop), :]
+
+    def to_plane(i):
+        own = term(targets[i] * rows + core * half)
         arrived(sib_in.at[i], tc_s.at[i], tc_r.at[i], sibling)
-        half_sum[i] = (own + sib_in[i].astype(jnp.float32)).astype(jnp.bfloat16)
-        for k in range(3):
+        half_sum[i] = own + sib_in[i].astype(jnp.float32)
+        for k in range(2):
+            first_out[i, k, :hop] = rows_of(i, chips[2], k).astype(jnp.bfloat16)
+            first_out[i, k, hop:] = rows_of(i, chips[k], k).astype(jnp.bfloat16)
             send(
-                at(half_sum.at[i], chips[k] * sub, sub),
-                plane_in.at[i, k],
-                tp_s.at[i, k],
-                tp_r.at[i, k],
-                peers[k],
+                first_out.at[i, k], first_in.at[i, k], tp_s.at[i, k], tp_r.at[i, k], peers[k]
             )
+
+    def second(i):
+        for k in range(2):
+            arrived(first_in.at[i, k], tp_s.at[i, k], tp_r.at[i, k], peers[k])
+            second_out[i, k] = (
+                rows_of(i, chips[1 - k], k) + first_in[i, k, :hop].astype(jnp.float32)
+            ).astype(jnp.bfloat16)
+            send(
+                second_out.at[i, k],
+                second_in.at[i, k],
+                tp_s.at[i, 2 + k],
+                tp_r.at[i, 2 + k],
+                peers[1 - k],
+            )
+
+    def third(i):
+        parts = []
+        for k in range(2):
+            arrived(second_in.at[i, k], tp_s.at[i, 2 + k], tp_r.at[i, 2 + k], peers[1 - k])
+            parts.append(
+                rows_of(i, chip, k)
+                + first_in[i, k, hop:].astype(jnp.float32)
+                + second_in[i, k].astype(jnp.float32)
+            )
+        if i == n_fsdp - 1:
+            return parts
+        for k in range(2):
+            shard_out[i, k * hop : (k + 1) * hop] = parts[k].astype(jnp.bfloat16)
+        send(shard_out.at[i], shard_in.at[i], tz_s.at[i], tz_r.at[i], (me, targets[i]))
+
     stores = []
-    for i, j in enumerate(order):
+
+    def input_rows(i):
         c0, c1 = i * rows, (i + 1) * rows
         ig[:, c0:c1] = (
             lax.dot_general(
@@ -197,33 +268,47 @@
         )
         store.start()
         stores.append(store)
-        acc = half_sum[i, pl.ds(pl.multiple_of(chip * sub, 16), sub), :].astype(jnp.float32)
-        for k in range(3):
-            arrived(plane_in.at[i, k], tp_s.at[i, k], tp_r.at[i, k], peers[k])
-            acc += plane_in[i, k].astype(jnp.float32)
-        if j:
-            shard_out[i] = acc.astype(jnp.bfloat16)
-            send(shard_out.at[i], shard_in.at[i], tz_s.at[i], tz_r.at[i], (me, above[j]))
+
+    for i in range(n_fsdp):
+        to_plane(i)
+    input_rows(0)
+    second(0)
+    input_rows(1)
+    second(1)
+    third(0)
+    input_rows(2)
+    second(2)
+    third(1)
+    input_rows(3)
+    second(3)
+    third(2)
+    parts = third(3)
     for i in range(n_fsdp - 1):
-        arrived(shard_in.at[i], tz_s.at[i], tz_r.at[i], (me, above[order[i]]))
-        acc += shard_in[i].astype(jnp.float32)
-
-    total[pl.ds(pl.multiple_of(mine, 16), sub), :] = acc.astype(jnp.bfloat16)
+        arrived(shard_in.at[i], tz_s.at[i], tz_r.at[i], (me, targets[i]))
+        for k in range(2):
+            parts[k] += shard_in[i, k * hop : (k + 1) * hop].astype(jnp.float32)
+
+    for k in range(2):
+        start = pl.multiple_of(mine + k * hop, 16)
+        total[pl.ds(start, hop), :] = parts[k].astype(jnp.bfloat16)
     piece = at(total, mine, sub)
-    for k in range(3):
+    for k in (2, 0, 1):
         send(piece, piece, gp_s.at[k], gp_r.at[k], peers[k])
     send(piece, piece, gc_s.at[3], gc_r.at[3], sibling)
-    for k in (1, 2, 0):
+    for k in range(3):
         piece = at(total, core * half + chips[k] * sub, sub)
         arrived(piece, gp_s.at[k], gp_r.at[k], peers[k])
         send(piece, piece, gc_s.at[k], gc_r.at[k], sibling)
-    for k in (3, 1, 2, 0):
+    for k in (3, 0, 1, 2):
         q = chip if k == 3 else chips[k]
         arrived(at(total, (1 - core) * half + q * sub, sub), gc_s.at[k], gc_r.at[k], sibling)
     last = pltpu.make_async_copy(total, g_hbm, local_sem.at[3 + n_fsdp])
     last.start()
     for copy in sent:
         copy.wait_send()
+    handed_on(z, z < n_fsdp - 1, z > 0)
+    for source in sources:
+        handed_on(source, *onward(source))
     for store in stores:
         store.wait()
     last.wait()
@@ -243,7 +328,7 @@
             jax.ShapeDtypeStruct((tok, width), bf),
             jax.ShapeDtypeStruct((rows, cols), bf),
         ),
-        in_specs=[anywhere] * 3,
+        in_specs=[pl.BlockSpec(memory_space=pltpu.HBM)] * 3,
         out_specs=(anywhere, anywhere),
         scratch_shapes=[
             pltpu.VMEM((tok, width), bf),
@@ -253,22 +338,25 @@
             pltpu.VMEM((tok, width), bf),
             pltpu.VMEM((n_fsdp, half, cols), bf),
             pltpu.VMEM((n_fsdp, half, cols), bf),
-            pltpu.VMEM((n_fsdp, half, cols), bf),
-            pltpu.VMEM((n_fsdp, 3, sub, cols), bf),
+            pltpu.VMEM((n_fsdp, half, cols), jnp.float32),
+            pltpu.VMEM((n_fsdp, 2, sub, cols), bf),
+            pltpu.VMEM((n_fsdp, 2, sub, cols), bf),
+            pltpu.VMEM((n_fsdp, 2, sub // 2, cols), bf),
+            pltpu.VMEM((n_fsdp, 2, sub // 2, cols), bf),
             pltpu.VMEM((s, sub, cols), bf),
             pltpu.VMEM((s, sub, cols), bf),
             pltpu.VMEM((rows, cols), bf),
             dma((4 + n_fsdp,)),
-            dma((s,)),
-            dma((s,)),
-            dma((s, 3)),
-            dma((s, 3)),
+            dma((2, n_fsdp)),
+            dma((n_fsdp,)),
+            dma((s, 4)),
+            dma((s, 4)),
             dma((s,)),
             dma((s,)),
             dma((n_fsdp,)),
             dma((n_fsdp,)),
-            dma((n_fsdp, 3)),
-            dma((n_fsdp, 3)),
+            dma((n_fsdp, 4)),
+            dma((n_fsdp, 4)),
             dma((s,)),
             dma((s,)),
             dma((3,)),
@@ -277,7 +365,7 @@
             dma((4,)),
         ],
         compiler_params=pltpu.CompilerParams(
-            collective_id=0, has_side_effects=True, vmem_limit_bytes=48 * 2**20
+            collective_id=0, has_side_effects=True, vmem_limit_bytes=61 * 2**20
         ),
         cost_estimate=pl.CostEstimate(
             flops=6 * tok * width * cols, bytes_accessed=4 * tok * width, transcendentals=0
@@ -308,7 +396,7 @@
     replicas = lax.axis_size("replica")
     n_fsdp = lax.axis_size("fsdp")
     rows = inner_weight.shape[0]
-    if replicas == 8 and rows % 256 == 0 and n_fsdp > 1:
+    if replicas == 8 and n_fsdp == 4 and rows % 256 == 0:
         input_grad, grad_sum = fused(acts, cotangent, inner_weight, n_fsdp)
     else:
         input_grad, grad_sum = by_collectives(acts, cotangent, inner_weight)

time: 71.9 us -> 69.7 us (0.969)
  local copies, waits for them, and re-layouts: 4.47 us -> 1.07 us
  other arithmetic: 2.94 us -> 4.95 us
    unnamed x11 -> x7, local copies, waits for them, and re-layouts: 4.47 us -> 1.07 us
    convert_element_type x1, other arithmetic: 2.94 us -> 4.95 us  [per_device(): return (input_grad, new_outer, new_momentum, new_outer.astype(jnp.bfloat16))]
where the time goes in v2:
time: 69.7 us; the launch traced here: 69.6 us
  Pallas kernels  62.9 us (90%)
  other arithmetic  4.95 us (7%)
  local copies, waits for them, and re-layouts  1.07 us (2%)
    pallas_call x1, Pallas kernels, fused(): pl.pallas_call(functools.partial(kernel, n_fsdp), out_shape=(jax.ShapeDty...  62.9 us
    convert_element_type x1, other arithmetic, per_device(): return (input_grad, new_outer, new_momentum, new_outer.astype(jnp.bfloat16))  4.95 us

profile of v2, /device:TPU:1, one launch (start us, length us, event | category | flops | bytes accessed | tf_op | source)
XLA Modules:
  0.0 69.6 jit_solution(16401260246046666231)
XLA Ops:
  0.6 0.0 copy-start.2
  0.6 0.0 copy-start
  0.7 62.9 %shard_map.84 = (bf16[128,5120]{1,0:T(8,128)(2,1)}, bf16[1280,384]{1,0:T(8,128)(2,1)}) custom-call(bf16[128,5120]{1,0:T(8,128)(2,1)} %acts_hbm.1, bf16[128,384]{1,0:T(8,128)(2,1)} %cot_hbm.1, bf16[1280,384]{1,0:T(8,128)(2,1)} %w_hbm.1), custom_call_target="tpu_custom_call" | custom-call | flops 1509949440 | bytes 2621440 | tf_op jit(solution)/shard_map/pallas_call | solution.py:325
  63.5 0.0 copy-done.2
  63.6 0.0 copy-done
  63.6 0.0 copy-start.1
  63.6 5.0 %fusion = (bf16[1280,384]{1,0:T(8,128)(2,1)}, f32[1280,384]{1,0:T(8,128)}, f32[1280,384]{1,0:T(8,128)}) fusion(f32[1280,384]{1,0:T(8,128)S(1)} %copy-done, bf16[1280,384]{1,0:T(8,128)(2,1)} %get-tuple-element.7, bf16[1280,384]{1,0:T(8,128)(2,1)S(1)} %copy-done.2, f32[1280,384]{1,0:T(8,128)} %param.9), kind=kLoop, calls=%fused_computation.3 | loop fusion | flops 5898240 | bytes 10813440 | tf_op jit(solution)/shard_map/convert_element_type | solution.py:407
  68.5 0.0 copy-done.1
  68.5 1.1 %copy.10 = bf16[128,5120]{1,0:T(8,128)(2,1)} copy(bf16[128,5120]{1,0:T(8,128)(2,1)S(1)} %copy-done.1) | data formatting | bytes 2621440
Async XLA Ops:
  0.6 62.9 %copy-start.2 = (bf16[1280,384]{1,0:T(8,128)(2,1)S(1)}, bf16[1280,384]{1,0:T(8,128)(2,1)}, u32[]{:S(2)}) copy-start(bf16[1280,384]{1,0:T(8,128)(2,1)} %w_hbm.1) | copy-start | bytes 2949124
  0.6 62.9 %copy-start = (f32[1280,384]{1,0:T(8,128)S(1)}, f32[1280,384]{1,0:T(8,128)}, u32[]{:S(2)}) copy-start(f32[1280,384]{1,0:T(8,128)} %param.8) | copy-start | bytes 5898244
  63.6 5.0 %copy-start.1 = (bf16[128,5120]{1,0:T(8,128)(2,1)S(1)}, bf16[128,5120]{1,0:T(8,128)(2,1)}, u32[]{:S(2)}) copy-start(bf16[128,5120]{1,0:T(8,128)(2,1)} %get-tuple-element.15) | copy-start | bytes 3932164

commit v3 on v2

--- a/solution.py
+++ b/solution.py
@@ -139,8 +139,13 @@
 
     mine = core * half + chip * sub
     hand_on(z, z < n_fsdp - 1, z > 0, at(w_hbm, mine, sub))
-    for load in loads:
-        load.wait()
+
+    def turn(b):
+        acts_t[b * half : (b + 1) * half, :] = acts[:, b * half : (b + 1) * half].T
+
+    loads[1].wait()
+    turn(0)
+    turn(1)
 
     def partial_pre(start, size):
         start = pl.multiple_of(start, 128)
@@ -159,8 +164,7 @@
         hand_on(source, *onward(source), piece)
         send(piece, piece, wp_s.at[t, 0], wp_r.at[t, 0], x_peer)
         send(piece, piece, wp_s.at[t, 1], wp_r.at[t, 1], y_peer)
-
-    pre = partial_pre(z * rows, rows)
+        turn(2 + t)
 
     def relay(t):
         start = sources[t] * rows + core * half
@@ -180,11 +184,16 @@
         send(piece, piece, wc_s.at[t], wc_r.at[t], sibling)
         return partial_pre(start, half)
 
+    loads[0].wait()
+    loads[2].wait()
     relay(0)
-    for b in range(width // half):
-        acts_t[b * half : (b + 1) * half, :] = acts[:, b * half : (b + 1) * half].T
+    pre = partial_pre(z * rows, half)
+    turn(5)
     relay(1)
     pre += use(0)
+    pre += partial_pre(z * rows + half, half)
+    for b in range(6, width // half):
+        turn(b)
     relay(2)
     pre += use(1)
     pre += use(2)
@@ -253,7 +262,7 @@
     stores = []
 
     def input_rows(i):
-        c0, c1 = i * rows, (i + 1) * rows
+        c0, c1 = i * half, (i + 1) * half
         ig[:, c0:c1] = (
             lax.dot_general(
                 grad_pre,
@@ -269,19 +278,22 @@
         store.start()
         stores.append(store)
 
-    for i in range(n_fsdp):
-        to_plane(i)
-    input_rows(0)
+    to_plane(0)
+    to_plane(1)
     second(0)
-    input_rows(1)
+    to_plane(2)
     second(1)
     third(0)
-    input_rows(2)
+    to_plane(3)
+    input_rows(0)
     second(2)
     third(1)
-    input_rows(3)
+    input_rows(1)
+    input_rows(2)
     second(3)
     third(2)
+    input_rows(3)
+    input_rows(4)
     parts = third(3)
     for i in range(n_fsdp - 1):
         arrived(shard_in.at[i], tz_s.at[i], tz_r.at[i], (me, targets[i]))
@@ -295,15 +307,27 @@
     for k in (2, 0, 1):
         send(piece, piece, gp_s.at[k], gp_r.at[k], peers[k])
     send(piece, piece, gc_s.at[3], gc_r.at[3], sibling)
+
+    def keep(slot, start):
+        store = pltpu.make_async_copy(
+            at(total, start, sub), at(g_hbm, start, sub), local_sem.at[3 + 8 + slot]
+        )
+        store.start()
+        stores.append(store)
+
+    keep(3, mine)
+    for i in range(5, width // half):
+        input_rows(i)
     for k in range(3):
-        piece = at(total, core * half + chips[k] * sub, sub)
+        start = core * half + chips[k] * sub
+        piece = at(total, start, sub)
         arrived(piece, gp_s.at[k], gp_r.at[k], peers[k])
         send(piece, piece, gc_s.at[k], gc_r.at[k], sibling)
+        keep(k, start)
     for k in (3, 0, 1, 2):
-        q = chip if k == 3 else chips[k]
-        arrived(at(total, (1 - core) * half + q * sub, sub), gc_s.at[k], gc_r.at[k], sibling)
-    last = pltpu.make_async_copy(total, g_hbm, local_sem.at[3 + n_fsdp])
-    last.start()
+        start = (1 - core) * half + (chip if k == 3 else chips[k]) * sub
+        arrived(at(total, start, sub), gc_s.at[k], gc_r.at[k], sibling)
+        keep(4 + k, start)
     for copy in sent:
         copy.wait_send()
     handed_on(z, z < n_fsdp - 1, z > 0)
@@ -311,7 +335,6 @@
         handed_on(source, *onward(source))
     for store in stores:
         store.wait()
-    last.wait()
 
 
 def fused(acts, cotangent, inner_weight, n_fsdp):
@@ -346,7 +369,7 @@
             pltpu.VMEM((s, sub, cols), bf),
             pltpu.VMEM((s, sub, cols), bf),
             pltpu.VMEM((rows, cols), bf),
-            dma((4 + n_fsdp,)),
+            dma((3 + 8 + 8,)),
             dma((2, n_fsdp)),
             dma((n_fsdp,)),
             dma((s, 4)),
@@ -365,7 +388,7 @@
             dma((4,)),
         ],
         compiler_params=pltpu.CompilerParams(
-            collective_id=0, has_side_effects=True, vmem_limit_bytes=61 * 2**20
+            collective_id=0, has_side_effects=True, vmem_limit_bytes=59 * 2**20
         ),
         cost_estimate=pl.CostEstimate(
             flops=6 * tok * width * cols, bytes_accessed=4 * tok * width, transcendentals=0

time: 69.7 us -> 66.1 us (0.948)
  Pallas kernels: 62.9 us -> 59.8 us
    pallas_call x1, Pallas kernels: 62.9 us -> 59.8 us  [fused(): pl.pallas_call(functools.partial(kernel, n_fsdp), out_shape=(jax.ShapeDty...]
where the time goes in v3:
time: 66.1 us; the launch traced here: 65.9 us
  Pallas kernels  59.8 us (90%)
  other arithmetic  4.31 us (7%)
  local copies, waits for them, and re-layouts  1.07 us (2%)
  between operations  0.7 us (1%)
    pallas_call x1, Pallas kernels, fused(): pl.pallas_call(functools.partial(kernel, n_fsdp), out_shape=(jax.ShapeDty...  59.8 us
    convert_element_type x1, other arithmetic, per_device(): return (input_grad, new_outer, new_momentum, new_outer.astype(jnp.bfloat16))  4.31 us

profile of v3, /device:TPU:1, one launch (start us, length us, event | category | flops | bytes accessed | tf_op | source)
XLA Modules:
  0.0 65.9 jit_solution(14228824721606811826)
XLA Ops:
  0.6 0.0 copy-start.3
  0.6 0.0 copy-start.1
  0.7 0.0 copy-start
  0.7 59.8 %shard_map.84 = (bf16[128,5120]{1,0:T(8,128)(2,1)}, bf16[1280,384]{1,0:T(8,128)(2,1)}) custom-call(bf16[128,5120]{1,0:T(8,128)(2,1)} %acts_hbm.1, bf16[128,384]{1,0:T(8,128)(2,1)} %cot_hbm.1, bf16[1280,384]{1,0:T(8,128)(2,1)} %w_hbm.1), custom_call_target="tpu_custom_call" | custom-call | flops 1509949440 | bytes 2621440 | tf_op jit(solution)/shard_map/pallas_call | solution.py:348
  60.5 0.0 copy-done.3
  60.5 0.0 copy-done.1
  60.5 0.0 copy-done
  60.5 0.0 copy-start.2
  60.5 4.3 %fusion = (bf16[1280,384]{1,0:T(8,128)(2,1)}, f32[1280,384]{1,0:T(8,128)}, f32[1280,384]{1,0:T(8,128)}) fusion(f32[1280,384]{1,0:T(8,128)S(1)} %copy-done, bf16[1280,384]{1,0:T(8,128)(2,1)} %get-tuple-element.7, bf16[1280,384]{1,0:T(8,128)(2,1)S(1)} %copy-done.3, f32[1280,384]{1,0:T(8,128)S(1)} %copy-done.1), kind=kLoop, calls=%fused_computation.3 | loop fusion | flops 5898240 | bytes 10813440 | tf_op jit(solution)/shard_map/convert_element_type | solution.py:430
  64.8 0.0 copy-done.2
  64.9 1.1 %copy.10 = bf16[128,5120]{1,0:T(8,128)(2,1)} copy(bf16[128,5120]{1,0:T(8,128)(2,1)S(1)} %copy-done.2) | data formatting | bytes 2621440
Async XLA Ops:
  0.6 59.9 %copy-start.3 = (bf16[1280,384]{1,0:T(8,128)(2,1)S(1)}, bf16[1280,384]{1,0:T(8,128)(2,1)}, u32[]{:S(2)}) copy-start(bf16[1280,384]{1,0:T(8,128)(2,1)} %w_hbm.1) | copy-start | bytes 2949124
  0.6 59.9 %copy-start.1 = (f32[1280,384]{1,0:T(8,128)S(1)}, f32[1280,384]{1,0:T(8,128)}, u32[]{:S(2)}) copy-start(f32[1280,384]{1,0:T(8,128)} %param.9) | copy-start | bytes 5898244
  0.7 59.9 %copy-start = (f32[1280,384]{1,0:T(8,128)S(1)}, f32[1280,384]{1,0:T(8,128)}, u32[]{:S(2)}) copy-start(f32[1280,384]{1,0:T(8,128)} %param.8) | copy-start | bytes 5898244
  60.5 4.3 %copy-start.2 = (bf16[128,5120]{1,0:T(8,128)(2,1)S(1)}, bf16[128,5120]{1,0:T(8,128)(2,1)}, u32[]{:S(2)}) copy-start(bf16[128,5120]{1,0:T(8,128)(2,1)} %get-tuple-element.15) | copy-start | bytes 3932164

commit v4 on v3

--- a/solution.py
+++ b/solution.py
@@ -164,6 +164,7 @@
         hand_on(source, *onward(source), piece)
         send(piece, piece, wp_s.at[t, 0], wp_r.at[t, 0], x_peer)
         send(piece, piece, wp_s.at[t, 1], wp_r.at[t, 1], y_peer)
+        send(piece, piece, wc_s.at[t, 3], wc_r.at[t, 3], sibling)
         turn(2 + t)
 
     def relay(t):
@@ -175,13 +176,24 @@
         piece = at(w_all, start + chips[1] * sub + hop, hop)
         send(piece, piece, wp_s.at[t, 2], wp_r.at[t, 2], x_peer)
 
+        for k in range(2):
+            piece = at(w_all, start + chips[k] * sub, sub)
+            send(piece, piece, wc_s.at[t, k], wc_r.at[t, k], sibling)
+
     def use(t):
         start = sources[t] * rows + core * half
         diagonal = start + chips[2] * sub
         arrived(at(w_all, diagonal, hop), wp_s.at[t, 3], wp_r.at[t, 3], y_peer)
         arrived(at(w_all, diagonal + hop, hop), wp_s.at[t, 2], wp_r.at[t, 2], x_peer)
-        piece = at(w_all, start, half)
-        send(piece, piece, wc_s.at[t], wc_r.at[t], sibling)
+        piece = at(w_all, diagonal, sub)
+        send(piece, piece, wc_s.at[t, 2], wc_r.at[t, 2], sibling)
+        return partial_pre(start, half)
+
+    def other_half(t):
+        start = sources[t] * rows + (1 - core) * half
+        for k, q in ((3, chip), (0, chips[0]), (1, chips[1]), (2, chips[2])):
+            piece = at(w_all, start + q * sub, sub)
+            arrived(piece, wc_s.at[t, k], wc_r.at[t, k], sibling)
         return partial_pre(start, half)
 
     loads[0].wait()
@@ -196,11 +208,10 @@
         turn(b)
     relay(2)
     pre += use(1)
+    pre += other_half(0)
     pre += use(2)
-    for t, source in enumerate(sources):
-        start = source * rows + (1 - core) * half
-        arrived(at(w_all, start, half), wc_s.at[t], wc_r.at[t], sibling)
-        pre += partial_pre(start, half)
+    pre += other_half(1)
+    pre += other_half(2)
 
     pre = pre * scale
     sig = jax.nn.sigmoid(pre)
@@ -212,8 +223,8 @@
         block = acts_t[pl.ds(pl.multiple_of(start, 128), half), :]
         return jnp.dot(block, grad_pre, preferred_element_type=jnp.float32) * scale
 
-    for i, target in enumerate(targets):
-        sib_out[i] = term(target * rows + (1 - core) * half).astype(jnp.bfloat16)
+    def to_sibling(i):
+        sib_out[i] = term(targets[i] * rows + (1 - core) * half).astype(jnp.bfloat16)
         send(sib_out.at[i], sib_in.at[i], tc_s.at[i], tc_r.at[i], sibling)
 
     def rows_of(i, q, second):
@@ -278,8 +289,12 @@
         store.start()
         stores.append(store)
 
+    to_sibling(0)
+    to_sibling(1)
     to_plane(0)
+    to_sibling(2)
     to_plane(1)
+    to_sibling(3)
     second(0)
     to_plane(2)
     second(1)
@@ -374,8 +389,8 @@
             dma((n_fsdp,)),
             dma((s, 4)),
             dma((s, 4)),
-            dma((s,)),
-            dma((s,)),
+            dma((s, 4)),
+            dma((s, 4)),
             dma((n_fsdp,)),
             dma((n_fsdp,)),
             dma((n_fsdp, 4)),

time: 66.1 us -> 64.8 us (0.980)
  Pallas kernels: 59.8 us -> 58.6 us
    pallas_call x1, Pallas kernels: 59.8 us -> 58.6 us  [fused(): pl.pallas_call(functools.partial(kernel, n_fsdp), out_shape=(jax.ShapeDty...]
where the time goes in v4:
time: 64.8 us; the launch traced here: 64.7 us
  Pallas kernels  58.6 us (90%)
  other arithmetic  4.31 us (7%)
  local copies, waits for them, and re-layouts  1.07 us (2%)
  between operations  0.7 us (1%)
    pallas_call x1, Pallas kernels, fused(): pl.pallas_call(functools.partial(kernel, n_fsdp), out_shape=(jax.ShapeDty...  58.6 us
    convert_element_type x1, other arithmetic, per_device(): return (input_grad, new_outer, new_momentum, new_outer.astype(jnp.bfloat16))  4.31 us

profile of v4, /device:TPU:1, one launch (start us, length us, event | category | flops | bytes accessed | tf_op | source)
XLA Modules:
  0.0 64.7 jit_solution(12613256304285843318)
XLA Ops:
  0.6 0.0 copy-start.3
  0.6 0.0 copy-start.1
  0.7 0.0 copy-start
  0.7 58.6 %shard_map.84 = (bf16[128,5120]{1,0:T(8,128)(2,1)}, bf16[1280,384]{1,0:T(8,128)(2,1)}) custom-call(bf16[128,5120]{1,0:T(8,128)(2,1)} %acts_hbm.1, bf16[128,384]{1,0:T(8,128)(2,1)} %cot_hbm.1, bf16[1280,384]{1,0:T(8,128)(2,1)} %w_hbm.1), custom_call_target="tpu_custom_call" | custom-call | flops 1509949440 | bytes 2621440 | tf_op jit(solution)/shard_map/pallas_call | solution.py:363
  59.2 0.0 copy-done.3
  59.2 0.0 copy-done.1
  59.3 0.0 copy-done
  59.3 0.0 copy-start.2
  59.3 4.3 %fusion = (bf16[1280,384]{1,0:T(8,128)(2,1)}, f32[1280,384]{1,0:T(8,128)}, f32[1280,384]{1,0:T(8,128)}) fusion(f32[1280,384]{1,0:T(8,128)S(1)} %copy-done, bf16[1280,384]{1,0:T(8,128)(2,1)} %get-tuple-element.7, bf16[1280,384]{1,0:T(8,128)(2,1)S(1)} %copy-done.3, f32[1280,384]{1,0:T(8,128)S(1)} %copy-done.1), kind=kLoop, calls=%fused_computation.3 | loop fusion | flops 5898240 | bytes 10813440 | tf_op jit(solution)/shard_map/convert_element_type | solution.py:445
  63.6 0.0 copy-done.2
  63.6 1.1 %copy.10 = bf16[128,5120]{1,0:T(8,128)(2,1)} copy(bf16[128,5120]{1,0:T(8,128)(2,1)S(1)} %copy-done.2) | data formatting | bytes 2621440
Async XLA Ops:
  0.6 58.6 %copy-start.3 = (bf16[1280,384]{1,0:T(8,128)(2,1)S(1)}, bf16[1280,384]{1,0:T(8,128)(2,1)}, u32[]{:S(2)}) copy-start(bf16[1280,384]{1,0:T(8,128)(2,1)} %w_hbm.1) | copy-start | bytes 2949124
  0.6 58.6 %copy-start.1 = (f32[1280,384]{1,0:T(8,128)S(1)}, f32[1280,384]{1,0:T(8,128)}, u32[]{:S(2)}) copy-start(f32[1280,384]{1,0:T(8,128)} %param.9) | copy-start | bytes 5898244
  0.7 58.6 %copy-start = (f32[1280,384]{1,0:T(8,128)S(1)}, f32[1280,384]{1,0:T(8,128)}, u32[]{:S(2)}) copy-start(f32[1280,384]{1,0:T(8,128)} %param.8) | copy-start | bytes 5898244
  59.3 4.3 %copy-start.2 = (bf16[128,5120]{1,0:T(8,128)(2,1)S(1)}, bf16[128,5120]{1,0:T(8,128)(2,1)}, u32[]{:S(2)}) copy-start(bf16[128,5120]{1,0:T(8,128)(2,1)} %get-tuple-element.15) | copy-start | bytes 3932164
